TPU v7x, 32 devices: a whole 2x2x4 slice. The times are simulated.
32 devices in a mesh: groups: 2 (over y), tensor: 16 (over z, x, core).
Axes of the slice: x: 2, y: 2, z: 4, core: 2. Of those that a mesh axis runs over, the one named last changes fastest.
Arguments:
- partials: bfloat16 [16, 256, 8192], P('tensor', 'groups'), parts along dimension 1, may hold values from -1000 to 1000
- norm_gain: float32 [8192], replicated, may hold values from 0.1 to 1.9
- head_weight: bfloat16 [8192, 9504], P(None, 'tensor'), may hold values from -30 to 30
- next_ids: int32 [256], P('groups'), parts along dimension 0, may hold values from 0 to 9503
- lengths: int32 [4], P('groups'), parts along dimension 0, may hold values from 16 to 64, as said below
Outputs:
- log_probs: bfloat16 [256, 9504], P(('groups', 'tensor')), parts along dimension 0
- target_logprob: float32 [256], P(('groups', 'tensor')), parts along dimension 0
There are 2 independent parts, one for each index of `groups`. A program takes and returns all parts, laid end to end along the dimension named above; an argument that names none is the same for every part. Nothing has to cross between parts.
Inputs may be any that keep to these rules, and one draw needn't show every extreme that they name: `lengths`: in every draw one micro-batch is full, with 64 valid positions.
All inputs are finite; a program needn't handle non-finite values.
Results may differ from a plain program's by a relative error of at most 0.004.
Values may be sent and summed in bfloat16 or wider, within the bound.
A program may use at most 64 MiB of HBM per device.

v0:
```python
import jax
import jax.numpy as jnp
from jax import lax
from jax.sharding import PartitionSpec as P

MB = 64


temper = 2.0


def valid_rows(count, lengths):
    position = jnp.arange(count, dtype=jnp.int32)
    batch = position // MB
    offset = position - batch * MB
    micro_ids = jnp.arange(lengths.shape[0], dtype=jnp.int32)
    limit = jnp.sum(jnp.where(batch[:, None] == micro_ids[None, :], lengths[None, :], 0), axis=1)
    return offset < limit


def rms_normed(hidden, norm_gain):
    scale = lax.rsqrt(jnp.mean(hidden * hidden, axis=1, keepdims=True) + 1e-06)
    return (hidden * scale * norm_gain).astype(jnp.bfloat16)


def on_device(partials, norm_gain, head_weight, next_ids, lengths):
    rows_all = partials.shape[1]
    own_rows = rows_all // lax.axis_size("tensor")
    first_row = lax.axis_index("tensor") * own_rows
    term = jnp.sum(partials, axis=0, dtype=jnp.float32)
    hidden = lax.psum(term, "tensor")
    normed = rms_normed(hidden, norm_gain)
    logits = jnp.dot(normed, head_weight, preferred_element_type=jnp.float32) / temper
    valid_all = valid_rows(rows_all, lengths)
    regrouped = lax.all_to_all(logits, "tensor", split_axis=0, concat_axis=1, tiled=True)
    top = jnp.max(regrouped, axis=1, keepdims=True)
    logsum = top + jnp.log(jnp.sum(jnp.exp(regrouped - top), axis=1, keepdims=True))
    logprob = regrouped - logsum
    ids_own = lax.dynamic_slice_in_dim(next_ids, first_row, own_rows)
    valid_own = lax.dynamic_slice_in_dim(valid_all, first_row, own_rows)
    columns = jnp.arange(regrouped.shape[1], dtype=jnp.int32)
    picked = jnp.sum(jnp.where(columns[None, :] == ids_own[:, None], logprob, 0.0), axis=1)
    log_probs = jnp.where(valid_own[:, None], logprob, 0.0).astype(jnp.bfloat16)
    target_logprob = jnp.where(valid_own, picked, 0.0)
    return (log_probs, target_logprob)


def solution(mesh):
    return jax.shard_map(
        on_device,
        mesh=mesh,
        in_specs=(P("tensor", "groups", None), P(), P(None, "tensor"), P("groups"), P("groups")),
        out_specs=(P(("groups", "tensor"), None), P(("groups", "tensor"))),
        check_vma=False,
    )
```

profile of v0, /device:TPU:0, one launch (start us, length us, event | category | flops | bytes accessed | tf_op | source)
XLA Modules:
  0.0 159.8 jit_solution(16426350399587039386)
XLA Ops:
  7.2 0.0 all-reduce.2.cloned.1.call-start
  7.2 4.0 %bitcast_convert_fusion = f32[128,8192]{1,0:T(8,128)} fusion(bf16[1,128,8192]{2,1,0:T(8,128)(2,1)} %param.5), kind=kLoop, calls=%fused_computation.3 | loop fusion | flops 1048576 | bytes 6291456 | tf_op jit(solution)/shard_map/reduce_sum | solution.py:30
  11.2 0.0 copy-start.1
  11.2 0.0 all-reduce.2.cloned.1.call-update
  11.2 114.5 %all-reduce.2.cloned.1.call-done = f32[128,8192]{1,0:T(8,128)} async-done(((f32[128,8192]{1,0:T(8,128)}), f32[128,8192]{1,0:T(8,128)}) %all-reduce.2.cloned.1.call-update) | async-done | bytes 4194320 | tf_op jit(solution)/shard_map/psum | solution.py:31
  125.7 0.0 copy-start
  125.7 2.7 %multiply_reduce_fusion = f32[128]{0:T(128)S(1)} fusion(f32[128,8192]{1,0:T(8,128)} %all-reduce.2.cloned.1.call-done), kind=kLoop, calls=%fused_computation.1 | loop fusion | flops 2097024 | bytes 4194816 | tf_op jit(solution)/shard_map/reduce_sum | solution.py:22
  128.4 0.0 copy-done.1
  128.5 0.7 copy-done
  129.2 0.0 copy-start.2
  129.2 0.0 copy-start.3
  129.2 5.8 %fusion.3 = f32[128,594]{0,1:T(8,128)S(1)} fusion(bf16[8192,594]{0,1:T(8,128)(2,1)} %param.7, f32[128,8192]{1,0:T(8,128)S(1)} %copy-done, f32[8192]{0:T(1024)S(1)} %copy-done.1, f32[128]{0:T(128)S(1)} %add_rsqrt_fusion), kind=kOutput, calls=%fused_computation.6 | convolution fusion | flops 1248930048 | bytes 14263808 | tf_op jit(solution)/shard_map/dot_general | solution.py:33
  135.0 0.9 copy.11
  135.9 3.6 %all-to-all-start = ((f32[16,8,594]{2,1,0:T(8,128)}), f32[16,8,594]{2,1,0:T(8,128)S(1)}, u32[]{:S(2)}, u32[]{:S(2)}) async-start(f32[16,8,594]{2,1,0:T(8,128)} %bitcast.1), calls=%async_computation | async-start | bytes 655360 | tf_op jit(solution)/shard_map/all_to_all | solution.py:35
  139.5 0.0 copy-done.2
  139.5 0.1 dynamic_slice.7
  139.6 0.0 copy-done.3
  139.6 0.1 fusion.4
  139.7 10.9 %all-to-all-done = f32[16,8,594]{2,1,0:T(8,128)S(1)} async-done(((f32[16,8,594]{2,1,0:T(8,128)}), f32[16,8,594]{2,1,0:T(8,128)S(1)}, u32[]{:S(2)}, u32[]{:S(2)}) %all-to-all-start) | async-done | bytes 304160 | tf_op jit(solution)/shard_map/all_to_all | solution.py:35
  150.6 0.2 reduce_max.9
  150.8 0.3 exponential_reduce_fusion
  151.1 0.1 copy.12
  151.2 0.2 all_to_all.17
  151.3 0.3 select_reduce_fusion
  151.6 0.6 broadcast_select_fusion
  152.2 0.8 select_convert_fusion
  (5 shorter events, 0.0 us)
Async XLA Ops:
  7.2 118.6 %all-reduce.2.cloned.1.call-start = ((), (), s32[]{:S(2)}) async-start(), calls=%async_computation.1 | async-start | bytes 8388608 | tf_op jit(solution)/shard_map/psum | solution.py:31
  11.2 117.3 %copy-start.1 = (f32[8192]{0:T(1024)S(1)}, f32[8192]{0:T(1024)}, u32[]{:S(2)}) copy-start(f32[8192]{0:T(1024)} %param.6) | copy-start | bytes 98308
  125.7 3.4 %copy-start = (f32[128,8192]{1,0:T(8,128)S(1)}, f32[128,8192]{1,0:T(8,128)}, u32[]{:S(2)}) copy-start(f32[128,8192]{1,0:T(8,128)} %all-reduce.2.cloned.1.call-done) | copy-start | bytes 12582916
  129.2 10.3 %copy-start.2 = (s32[128]{0:T(128)S(1)}, s32[128]{0:T(128)}, u32[]{:S(2)}) copy-start(s32[128]{0:T(128)} %param.8) | copy-start | bytes 1540
  129.2 10.4 %copy-start.3 = (s32[2]{0:T(128)S(1)}, s32[2]{0:T(128)}, u32[]{:S(2)}) copy-start(s32[2]{0:T(128)} %param.9) | copy-start | bytes 28
  135.9 14.7 %all-to-all-start = ((f32[16,8,594]{2,1,0:T(8,128)}), f32[16,8,594]{2,1,0:T(8,128)S(1)}, u32[]{:S(2)}, u32[]{:S(2)}) async-start(f32[16,8,594]{2,1,0:T(8,128)} %bitcast.1), calls=%async_computation | async-start | bytes 655360 | tf_op jit(solution)/shard_map/all_to_all | solution.py:35
Sparse Core Ops, SparseCore 0:
  11.7 114.0 all-reduce.1
where the time goes:
time: 160 us
  waiting for transfers between devices  125 us (78%)
  between operations  14.1 us (9%)
  other arithmetic  8.89 us (6%)
  matrix products  5.78 us (4%)
  starting transfers between devices  3.68 us (2%)
  local copies, waits for them, and re-layouts  1.95 us (1%)
    psum x1, waiting for transfers between devices, on_device(): hidden = lax.psum(term, 'tensor')  115 us
    all_to_all x1, waiting for transfers between devices, on_device(): lax.all_to_all(logits, 'tensor', split_axis=0, concat_axis=1, tiled=True)  10.9 us
    dot_general x1, matrix products, on_device(): jnp.dot(normed, head_weight, preferred_element_type=jnp.float32) / temper  5.78 us
    reduce_sum x1, other arithmetic, on_device(): term = jnp.sum(partials, axis=0, dtype=jnp.float32)  3.99 us
    all_to_all x1, starting transfers between devices, on_device(): lax.all_to_all(logits, 'tensor', split_axis=0, concat_axis=1, tiled=True)  3.64 us
  transfers between devices with their start and end apart: 2, of which 2 were waited for; matrix products, arithmetic and copies ran while one was open for 0% of the time, Pallas kernels for 0%

commit v1 on v0

--- a/solution.py
+++ b/solution.py
@@ -1,6 +1,9 @@
+import functools
 import jax
 import jax.numpy as jnp
 from jax import lax
+from jax.experimental import pallas as pl
+from jax.experimental.pallas import tpu as pltpu
 from jax.sharding import PartitionSpec as P
 
 MB = 64
@@ -23,7 +26,7 @@
     return (hidden * scale * norm_gain).astype(jnp.bfloat16)
 
 
-def on_device(partials, norm_gain, head_weight, next_ids, lengths):
+def on_device_plain(partials, norm_gain, head_weight, next_ids, lengths):
     rows_all = partials.shape[1]
     own_rows = rows_all // lax.axis_size("tensor")
     first_row = lax.axis_index("tensor") * own_rows
@@ -45,6 +48,294 @@
     return (log_probs, target_logprob)
 
 
+HALVES = 2
+
+
+def head_kernel(n, X, Z, part_ref, gain_ref, w_ref, ids_ref, len_ref, out_ref, tgt_ref,
+                pv, wv, rc, xs, xr, zs, zr, hb, acc, oacc, ssq, dbuf, frecv, sbuf, srecv,
+                loc_sem, c_ss, c_rs, x_ss, x_rs, z_ss, z_rs, gz_ss, gz_rs, gx_ss, gx_rs, gc_ss, gc_rs,
+                f_ss, f_rs, s_ss, s_rs):
+    f32 = jnp.float32
+    me = lax.axis_index("tensor")
+    c = lax.rem(me, 2)
+    x = lax.rem(lax.div(me, 2), X)
+    z = lax.div(me, 2 * X)
+    T, half = pv.shape
+    F = half // (X * Z)
+    TH = T // HALVES
+    N, D = wv.shape
+    own = out_ref.shape[0]
+
+    def dev(zz, xx, cc):
+        return {"tensor": (zz * X + xx) * 2 + cc}
+
+    def place(cc, xx, zz):
+        return (cc * X + xx) * Z + zz
+
+    def up(v, k, m):
+        return lax.rem(v + k, m)
+
+    def down(v, k, m):
+        return lax.rem(v + m - k, m)
+
+    def remote(src, dst, ss, rs, to):
+        return pltpu.make_async_remote_copy(src_ref=src, dst_ref=dst, send_sem=ss, recv_sem=rs, device_id=to,
+                                            device_id_type=pl.DeviceIdType.MESH)
+
+    core_dev = dev(z, x, 1 - c)
+    w_copy = pltpu.make_async_copy(w_ref, wv, loc_sem.at[0])
+    p_copy = pltpu.make_async_copy(part_ref.at[0, :, pl.ds(pl.multiple_of(c * half, half), half)], pv, loc_sem.at[1])
+    p_copy.start()
+    w_copy.start()
+
+    barrier = pltpu.get_barrier_semaphore()
+    for j in range(1, n):
+        pl.semaphore_signal(barrier, inc=1, device_id={"tensor": up(me, j, n)}, device_id_type=pl.DeviceIdType.MESH)
+    pl.semaphore_wait(barrier, n - 1)
+
+    sent = []
+
+    def go(copy):
+        copy.start()
+        sent.append(copy)
+
+    def rows(h):
+        return pl.ds(h * TH, TH)
+
+    wide = Z * F
+    for h in range(HALVES):
+        for j in range(X):
+            xx = up(x, 1 + j, X)
+            src = part_ref.at[0, rows(h), pl.ds(pl.multiple_of((1 - c) * half + xx * wide, wide), wide)]
+            dst = rc.at[rows(h), pl.ds(pl.multiple_of(xx * wide, wide), wide)]
+            go(remote(src, dst, c_ss.at[h, j], c_rs.at[h, j], core_dev))
+    p_copy.wait()
+
+    def core_wait(h, j):
+        dst = rc.at[rows(h), pl.ds(pl.multiple_of(up(x, 1 + j, X) * wide, wide), wide)]
+        remote(dst, dst, c_ss.at[h, j], c_rs.at[h, j], core_dev).wait_recv()
+
+    order = sorted(range(1, Z), key=lambda k: abs(k - Z // 2)) + [0]
+
+    def pair_sum(h, xx, zz):
+        cols = pl.ds(pl.multiple_of((xx * Z + zz) * F, F), F)
+        return pv[rows(h), cols].astype(f32) + rc[rows(h), cols].astype(f32)
+
+    def reduce_x(h):
+        for j in range(X - 1):
+            xx = up(x, 1 + j, X)
+            core_wait(h, j)
+            for k in order:
+                zz = up(z, k, Z)
+                xs[xx, zz, rows(h)] = pair_sum(h, xx, zz).astype(jnp.bfloat16)
+                go(remote(xs.at[xx, zz, rows(h)], xr.at[x, zz, rows(h)], x_ss.at[h, j, k], x_rs.at[h, j, k], dev(z, xx, c)))
+
+    def reduce_z(h, ks):
+        if ks[0] == order[0]:
+            core_wait(h, X - 1)
+        for k in ks:
+            zz = up(z, k, Z)
+            total = pair_sum(h, x, zz)
+            for j in range(X - 1):
+                xx = down(x, 1 + j, X)
+                got = xr.at[xx, zz, rows(h)]
+                remote(got, got, x_ss.at[h, j, k], x_rs.at[h, j, k], core_dev).wait_recv()
+                total = total + xr[xx, zz, rows(h)].astype(f32)
+            if k == 0:
+                oacc[rows(h)] = total
+            else:
+                zs[zz, rows(h)] = total.astype(jnp.bfloat16)
+                go(remote(zs.at[zz, rows(h)], zr.at[z, rows(h)], z_ss.at[h, k], z_rs.at[h, k], dev(zz, x, c)))
+
+    def spread(h, p, xo, k):
+        piece = hb.at[p, rows(h)]
+        go(remote(piece, piece, gc_ss.at[h, xo, k], gc_rs.at[h, xo, k], core_dev))
+
+    def spread_x(h, p, k):
+        piece = hb.at[p, rows(h)]
+        for j in range(X - 1):
+            go(remote(piece, piece, gx_ss.at[h, j, k], gx_rs.at[h, j, k], dev(z, up(x, 1 + j, X), c)))
+
+    def reduce_end(h):
+        total = oacc[rows(h)]
+        for k in order[:-1]:
+            zz = down(z, k, Z)
+            got = zr.at[zz, rows(h)]
+            remote(got, got, z_ss.at[h, k], z_rs.at[h, k], core_dev).wait_recv()
+            total = total + zr[zz, rows(h)].astype(f32)
+        p = place(c, x, z)
+        hb[p, rows(h)] = (total * gain_ref[:, pl.ds(pl.multiple_of(p * F, F), F)]).astype(jnp.bfloat16)
+        piece = hb.at[p, rows(h)]
+        for k in order[:-1]:
+            go(remote(piece, piece, gz_ss.at[h, k], gz_rs.at[h, k], dev(up(z, k, Z), x, c)))
+        spread_x(h, p, 0)
+        spread(h, p, 0, 0)
+
+    def gather_z(h):
+        for k in order[:-1]:
+            p = place(c, x, down(z, k, Z))
+            piece = hb.at[p, rows(h)]
+            remote(piece, piece, gz_ss.at[h, k], gz_rs.at[h, k], core_dev).wait_recv()
+            spread_x(h, p, k)
+            spread(h, p, 0, k)
+
+    def gather_x(h):
+        for k in [0] + order[:-1]:
+            for j in range(X - 1):
+                p = place(c, down(x, 1 + j, X), down(z, k, Z))
+                piece = hb.at[p, rows(h)]
+                remote(piece, piece, gx_ss.at[h, j, k], gx_rs.at[h, j, k], core_dev).wait_recv()
+                spread(h, p, 1 + j, k)
+
+    def multiply(h, from_core):
+        cc = 1 - c if from_core else c
+
+        def body(i, carry):
+            xo = lax.div(i, Z)
+            k = lax.rem(i, Z)
+            p = place(cc, down(x, xo, X), down(z, k, Z))
+            if from_core:
+                piece = hb.at[p, rows(h)]
+                remote(piece, piece, gc_ss.at[h, xo, k], gc_rs.at[h, xo, k], core_dev).wait_recv()
+            start = pl.multiple_of(p * F, F)
+            block = hb[p, rows(h)]
+            acc[rows(h)] += lax.dot_general(block, wv[:, pl.ds(start, F)], (((1,), (1,)), ((), ())),
+                                             preferred_element_type=f32)
+            plain = block.astype(f32) * (1.0 / gain_ref[:, pl.ds(start, F)])
+            square = plain * plain
+            part = square[:, :128]
+            for s in range(128, F, 128):
+                part = part + square[:, s:s + 128]
+            ssq[rows(h)] += part
+            return carry
+
+        lax.fori_loop(0, X * Z, body, 0)
+
+    def final_copies(s):
+        return (remote(dbuf.at[s], frecv.at[me], f_ss.at[s], f_rs.at[me], {"tensor": jnp.int32(s)}),
+                remote(sbuf.at[s], srecv.at[me], s_ss.at[s], s_rs.at[me], {"tensor": jnp.int32(s)}))
+
+    def finish(h):
+        scale = lax.rsqrt(jnp.sum(ssq[rows(h)], axis=1, keepdims=True) * (1.0 / D) + 1e-06) * (1.0 / temper)
+        logits = acc[rows(h)] * scale
+        top = jnp.max(logits, axis=1, keepdims=True)
+        low = logits - top
+        total = jnp.sum(jnp.exp(low), axis=1, keepdims=True)
+        ids = ids_ref[:, :].astype(f32)
+        r = lax.broadcasted_iota(jnp.int32, (TH, T), 0) + h * TH
+        t = lax.broadcasted_iota(jnp.int32, (TH, T), 1)
+        ids = jnp.sum(jnp.where(r == t, ids, 0.0), axis=1, keepdims=True).astype(jnp.int32)
+        column = lax.broadcasted_iota(jnp.int32, (TH, N), 1) + me * N
+        pick = jnp.sum(jnp.where(column == ids, logits, 0.0), axis=1, keepdims=True)
+        lane = lax.broadcasted_iota(jnp.int32, (TH, 128), 1)
+        stat = jnp.where(lane == 0, top, jnp.where(lane == 1, total, pick))
+        for i in range(TH // own):
+            s = h * (TH // own) + i
+            mine = low[i * own:(i + 1) * own].astype(jnp.bfloat16)
+            facts = stat[i * own:(i + 1) * own]
+            dbuf[s] = mine
+            sbuf[s] = facts
+
+            @pl.when(me != s)
+            def _():
+                for copy in final_copies(s):
+                    copy.start()
+
+            @pl.when(me == s)
+            def _():
+                frecv[s] = mine
+                srecv[s] = facts
+
+    acc[...] = jnp.zeros_like(acc)
+    ssq[...] = jnp.zeros_like(ssq)
+    reduce_x(0)
+    reduce_x(1)
+    reduce_z(0, order)
+    reduce_z(1, order[:1])
+    reduce_end(0)
+    reduce_z(1, order[1:])
+    gather_z(0)
+    reduce_end(1)
+    gather_x(0)
+    w_copy.wait()
+    multiply(0, False)
+    gather_z(1)
+    multiply(0, True)
+    finish(0)
+    gather_x(1)
+    multiply(1, False)
+    multiply(1, True)
+    finish(1)
+
+    for s in range(n):
+        @pl.when(me != s)
+        def _():
+            remote(frecv.at[s], frecv.at[s], f_ss.at[s], f_rs.at[s], core_dev).wait_recv()
+            remote(srecv.at[s], srecv.at[s], s_ss.at[s], s_rs.at[s], core_dev).wait_recv()
+
+    tops = [srecv[s][:, 0:1] for s in range(n)]
+    top = functools.reduce(jnp.maximum, tops)
+    total = sum(srecv[s][:, 1:2] * jnp.exp(tops[s] - top) for s in range(n))
+    pick = sum(srecv[s][:, 2:3] for s in range(n))
+    logsum = top + jnp.log(total)
+    position = lax.broadcasted_iota(jnp.int32, (own, 1), 0) + me * own
+    batch = lax.div(position, MB)
+    limit = jnp.zeros((own, 1), jnp.int32)
+    for m in range(T // MB):
+        limit = jnp.where(batch == m, len_ref[m], limit)
+    valid = position - batch * MB < limit
+    for s in range(n):
+        value = frecv[s].astype(f32) + (tops[s] - logsum)
+        out_ref[:, s * N:(s + 1) * N] = jnp.where(valid, value, 0.0).astype(jnp.bfloat16)
+    target = jnp.where(valid, pick - logsum, 0.0)
+    r = lax.broadcasted_iota(jnp.int32, (own, own), 0)
+    t = lax.broadcasted_iota(jnp.int32, (own, own), 1)
+    tgt_ref[...] = jnp.sum(jnp.where(r == t, target, 0.0), axis=0, keepdims=True)
+
+    for copy in sent:
+        copy.wait_send()
+    for s in range(n):
+        @pl.when(me != s)
+        def _():
+            for copy in final_copies(s):
+                copy.wait_send()
+
+
+def on_device(partials, norm_gain, head_weight, next_ids, lengths):
+    n = lax.axis_size("tensor")
+    terms, T, D = partials.shape
+    N = head_weight.shape[1]
+    own = T // n
+    F = D // n
+    if terms != 1 or F % 128 or own % 8 or n & (n - 1) or T % (MB * HALVES):
+        return on_device_plain(partials, norm_gain, head_weight, next_ids, lengths)
+    X = 1 << (((n // 2).bit_length() - 1) // 3)
+    Z = n // 2 // X
+    H = HALVES
+    bf16, f32 = jnp.bfloat16, jnp.float32
+    dma = pltpu.SemaphoreType.DMA
+    vmem = pl.BlockSpec(memory_space=pltpu.VMEM)
+    hbm = pl.BlockSpec(memory_space=pl.ANY)
+    sems = [(2,)] + [(H, X)] * 2 + [(H, X, Z)] * 2 + [(H, Z)] * 4 + [(H, X, Z)] * 4 + [(n,)] * 4
+    out, target = pl.pallas_call(
+        functools.partial(head_kernel, n, X, Z),
+        out_shape=(jax.ShapeDtypeStruct((own, n * N), bf16), jax.ShapeDtypeStruct((1, own), f32)),
+        in_specs=[hbm, vmem, hbm, vmem, pl.BlockSpec(memory_space=pltpu.SMEM)],
+        out_specs=(vmem, vmem),
+        scratch_shapes=[
+            pltpu.VMEM((T, D // 2), bf16), pltpu.VMEM((N, D), bf16), pltpu.VMEM((T, D // 2), bf16),
+            pltpu.VMEM((X, Z, T, F), bf16), pltpu.VMEM((X, Z, T, F), bf16),
+            pltpu.VMEM((Z, T, F), bf16), pltpu.VMEM((Z, T, F), bf16), pltpu.VMEM((n, T, F), bf16),
+            pltpu.VMEM((T, N), f32), pltpu.VMEM((T, F), f32), pltpu.VMEM((T, 128), f32),
+            pltpu.VMEM((n, own, N), bf16), pltpu.VMEM((n, own, N), bf16),
+            pltpu.VMEM((n, own, 128), f32), pltpu.VMEM((n, own, 128), f32),
+        ] + [dma(shape) for shape in sems],
+        compiler_params=pltpu.CompilerParams(collective_id=0, has_side_effects=True, vmem_limit_bytes=48 << 20),
+        cost_estimate=pl.CostEstimate(flops=2 * T * D * N, bytes_accessed=2 * D * (T + N), transcendentals=T * N),
+    )(partials, norm_gain[None, :], head_weight.T, next_ids[None, :], lengths)
+    return out, target.reshape(own)
+
+
 def solution(mesh):
     return jax.shard_map(
         on_device,

time: 160 us -> 56.9 us (0.36)
  waiting for transfers between devices: 125 us -> 0 us
  Pallas kernels: 0 us -> 51.2 us
  between operations: 14.1 us -> 0.65 us
  other arithmetic: 8.89 us -> 0 us
  matrix products: 5.78 us -> 0 us
  starting transfers between devices: 3.68 us -> 0 us
  local copies, waits for them, and re-layouts: 1.95 us -> 4.83 us
    psum x1 -> x0, waiting for transfers between devices: 115 us -> none  [on_device(): hidden = lax.psum(term, 'tensor')]
    pallas_call x0 -> x1, Pallas kernels: none -> 51.2 us  [on_device(): pl.pallas_call(functools.partial(head_kernel, n, X, Z), out_shape=(jax.Sh...]
    all_to_all x1 -> x0, waiting for transfers between devices: 10.9 us -> none  [on_device(): lax.all_to_all(logits, 'tensor', split_axis=0, concat_axis=1, tiled=True)]
    reduce_sum x5 -> x0, other arithmetic: 7.31 us -> none  [the longest x1 3.99 us: on_device(): term = jnp.sum(partials, axis=0, dtype=jnp.float32)]
    dot_general x1 -> x0, matrix products: 5.78 us -> none  [on_device(): jnp.dot(normed, head_weight, preferred_element_type=jnp.float32) / temper]
    unnamed x8 -> x10, local copies, waits for them, and re-layouts: 0.75 us -> 4.83 us
    all_to_all x1 -> x0, starting transfers between devices: 3.64 us -> none  [on_device(): lax.all_to_all(logits, 'tensor', split_axis=0, concat_axis=1, tiled=True)]
  transfers between devices with their start and end apart: 2 -> 0, of which waited for: 2 -> 0; matrix products, arithmetic and copies ran while one was open for 0% -> 0% of each run, Pallas kernels for 0% -> 0%
where the time goes in v1:
time: 56.9 us; the launch traced here: 56.6 us
  Pallas kernels  51.2 us (90%)
  local copies, waits for them, and re-layouts  4.83 us (8%)
  between operations  0.65 us (1%)
    pallas_call x1, Pallas kernels, on_device(): pl.pallas_call(functools.partial(head_kernel, n, X, Z), out_shape=(jax.Sh...  51.2 us
    unnamed x10, local copies, waits for them, and re-layouts  4.83 us

profile of v1, /device:TPU:0, one launch (start us, length us, event | category | flops | bytes accessed | tf_op | source)
XLA Modules:
  0.0 56.6 jit_solution(10437843662212462817)
XLA Ops:
  0.6 0.0 copy-start
  0.6 1.6 %copy-done = bf16[1,128,8192]{2,1,0:T(8,128)(2,1)S(1)} copy-done((bf16[1,128,8192]{2,1,0:T(8,128)(2,1)S(1)}, bf16[1,128,8192]{2,1,0:T(8,128)(2,1)}, u32[]{:S(2)}) %copy-start) | copy-done | bytes 2097176
  2.2 0.0 copy-start.1
  2.2 0.8 %copy-done.1 = f32[8192]{0:T(1024)S(1)} copy-done((f32[8192]{0:T(1024)S(1)}, f32[8192]{0:T(1024)}, u32[]{:S(2)}) %copy-start.1) | copy-done | bytes 32792
  3.0 0.0 copy-start.2
  3.0 0.7 %copy-done.2 = s32[128]{0:T(128)S(1)} copy-done((s32[128]{0:T(128)S(1)}, s32[128]{0:T(128)}, u32[]{:S(2)}) %copy-start.2) | copy-done | bytes 536
  3.6 0.0 copy-start.3
  3.6 0.7 %copy-done.3 = s32[2]{0:T(128)S(1)} copy-done((s32[2]{0:T(128)S(1)}, s32[2]{0:T(128)}, u32[]{:S(2)}) %copy-start.3) | copy-done | bytes 32
  4.3 51.2 %shard_map.68 = (bf16[8,9504]{1,0:T(8,128)(2,1)S(1)}, f32[1,8]{1,0:T(1,128)S(1)}) custom-call(bf16[1,128,8192]{2,1,0:T(8,128)(2,1)S(1)} %copy-done, f32[1,8192]{1,0:T(1,128)S(1)} %bitcast.4, bf16[594,8192]{1,0:T(8,128)(2,1)} %bitcast.7, s32[1,128]{1,0:T(1,128)S(1)} %bitcast.5, s32[2]{0:T(128)S(1)} %copy-done.3), custom_call_target="tpu_custom_call" | custom-call | flops 1245708288 | bytes 11829248 | tf_op jit(solution)/shard_map/pallas_call | solution.py:320
  55.5 0.7 %copy.9 = bf16[8,9504]{1,0:T(8,128)(2,1)} copy(bf16[8,9504]{1,0:T(8,128)(2,1)S(1)} %get-tuple-element.8) | data formatting | bytes 304128
  56.1 0.5 copy.10
Async XLA Ops:
  0.6 1.6 %copy-start = (bf16[1,128,8192]{2,1,0:T(8,128)(2,1)S(1)}, bf16[1,128,8192]{2,1,0:T(8,128)(2,1)}, u32[]{:S(2)}) copy-start(bf16[1,128,8192]{2,1,0:T(8,128)(2,1)} %part_ref.1) | copy-start | bytes 6291460
  2.2 0.8 %copy-start.1 = (f32[8192]{0:T(1024)S(1)}, f32[8192]{0:T(1024)}, u32[]{:S(2)}) copy-start(f32[8192]{0:T(1024)} %param.6) | copy-start | bytes 98308
  3.0 0.7 %copy-start.2 = (s32[128]{0:T(128)S(1)}, s32[128]{0:T(128)}, u32[]{:S(2)}) copy-start(s32[128]{0:T(128)} %param.8) | copy-start | bytes 1540
  3.6 0.7 %copy-start.3 = (s32[2]{0:T(128)S(1)}, s32[2]{0:T(128)}, u32[]{:S(2)}) copy-start(s32[2]{0:T(128)} %len_ref.1) | copy-start | bytes 28

commit v2 on v1

--- a/solution.py
+++ b/solution.py
@@ -49,6 +49,8 @@
 
 
 HALVES = 2
+CHUNKS = 4
+LAGS = (0, 1, 2, 3)
 
 
 def head_kernel(n, X, Z, part_ref, gain_ref, w_ref, ids_ref, len_ref, out_ref, tgt_ref,
@@ -63,6 +65,8 @@
     T, half = pv.shape
     F = half // (X * Z)
     TH = T // HALVES
+    TC = T // CHUNKS
+    per = CHUNKS // HALVES
     N, D = wv.shape
     own = out_ref.shape[0]
 
@@ -100,11 +104,13 @@
         sent.append(copy)
 
     def rows(h):
-        return pl.ds(h * TH, TH)
+        return pl.ds(h * TC, TC)
+
+    def half_rows(g):
+        return pl.ds(g * TH, TH)
 
     wide = Z * F
-    for h in range(HALVES):
-        for j in range(X):
+    for j, h in [(j, h) for j in range(X - 1) for h in range(CHUNKS)] + [(X - 1, h) for h in range(CHUNKS)]:
             xx = up(x, 1 + j, X)
             src = part_ref.at[0, rows(h), pl.ds(pl.multiple_of((1 - c) * half + xx * wide, wide), wide)]
             dst = rc.at[rows(h), pl.ds(pl.multiple_of(xx * wide, wide), wide)]
@@ -187,7 +193,7 @@
                 remote(piece, piece, gx_ss.at[h, j, k], gx_rs.at[h, j, k], core_dev).wait_recv()
                 spread(h, p, 1 + j, k)
 
-    def multiply(h, from_core):
+    def multiply(g, from_core):
         cc = 1 - c if from_core else c
 
         def body(i, carry):
@@ -195,18 +201,19 @@
             k = lax.rem(i, Z)
             p = place(cc, down(x, xo, X), down(z, k, Z))
             if from_core:
-                piece = hb.at[p, rows(h)]
-                remote(piece, piece, gc_ss.at[h, xo, k], gc_rs.at[h, xo, k], core_dev).wait_recv()
+                for h in range(g * per, (g + 1) * per):
+                    piece = hb.at[p, rows(h)]
+                    remote(piece, piece, gc_ss.at[h, xo, k], gc_rs.at[h, xo, k], core_dev).wait_recv()
             start = pl.multiple_of(p * F, F)
-            block = hb[p, rows(h)]
-            acc[rows(h)] += lax.dot_general(block, wv[:, pl.ds(start, F)], (((1,), (1,)), ((), ())),
+            block = hb[p, half_rows(g)]
+            acc[half_rows(g)] += lax.dot_general(block, wv[:, pl.ds(start, F)], (((1,), (1,)), ((), ())),
                                              preferred_element_type=f32)
             plain = block.astype(f32) * (1.0 / gain_ref[:, pl.ds(start, F)])
             square = plain * plain
             part = square[:, :128]
             for s in range(128, F, 128):
                 part = part + square[:, s:s + 128]
-            ssq[rows(h)] += part
+            ssq[half_rows(g)] += part
             return carry
 
         lax.fori_loop(0, X * Z, body, 0)
@@ -216,8 +223,8 @@
                 remote(sbuf.at[s], srecv.at[me], s_ss.at[s], s_rs.at[me], {"tensor": jnp.int32(s)}))
 
     def finish(h):
-        scale = lax.rsqrt(jnp.sum(ssq[rows(h)], axis=1, keepdims=True) * (1.0 / D) + 1e-06) * (1.0 / temper)
-        logits = acc[rows(h)] * scale
+        scale = lax.rsqrt(jnp.sum(ssq[half_rows(h)], axis=1, keepdims=True) * (1.0 / D) + 1e-06) * (1.0 / temper)
+        logits = acc[half_rows(h)] * scale
         top = jnp.max(logits, axis=1, keepdims=True)
         low = logits - top
         total = jnp.sum(jnp.exp(low), axis=1, keepdims=True)
@@ -248,24 +255,24 @@
 
     acc[...] = jnp.zeros_like(acc)
     ssq[...] = jnp.zeros_like(ssq)
-    reduce_x(0)
-    reduce_x(1)
-    reduce_z(0, order)
-    reduce_z(1, order[:1])
-    reduce_end(0)
-    reduce_z(1, order[1:])
-    gather_z(0)
-    reduce_end(1)
-    gather_x(0)
-    w_copy.wait()
-    multiply(0, False)
-    gather_z(1)
-    multiply(0, True)
-    finish(0)
-    gather_x(1)
-    multiply(1, False)
-    multiply(1, True)
-    finish(1)
+    for h in range(CHUNKS):
+        reduce_x(h)
+    stages = (lambda h: reduce_z(h, order), reduce_end, gather_z, gather_x)
+    for step in range(CHUNKS + LAGS[-1]):
+        for stage, lag in zip(stages, LAGS):
+            if 0 <= step - lag < CHUNKS:
+                stage(step - lag)
+        done = step - LAGS[-1] + 1
+        if done == per:
+            w_copy.wait()
+            multiply(0, False)
+        if done == per + 1:
+            multiply(0, True)
+            finish(0)
+    for g in range(1, HALVES):
+        multiply(g, False)
+        multiply(g, True)
+        finish(g)
 
     for s in range(n):
         @pl.when(me != s)
@@ -307,11 +314,11 @@
     N = head_weight.shape[1]
     own = T // n
     F = D // n
-    if terms != 1 or F % 128 or own % 8 or n & (n - 1) or T % (MB * HALVES):
+    if terms != 1 or F % 128 or own % 8 or n & (n - 1) or T % (16 * CHUNKS):
         return on_device_plain(partials, norm_gain, head_weight, next_ids, lengths)
     X = 1 << (((n // 2).bit_length() - 1) // 3)
     Z = n // 2 // X
-    H = HALVES
+    H = CHUNKS
     bf16, f32 = jnp.bfloat16, jnp.float32
     dma = pltpu.SemaphoreType.DMA
     vmem = pl.BlockSpec(memory_space=pltpu.VMEM)
@@ -330,7 +337,7 @@
             pltpu.VMEM((n, own, N), bf16), pltpu.VMEM((n, own, N), bf16),
             pltpu.VMEM((n, own, 128), f32), pltpu.VMEM((n, own, 128), f32),
         ] + [dma(shape) for shape in sems],
-        compiler_params=pltpu.CompilerParams(collective_id=0, has_side_effects=True, vmem_limit_bytes=48 << 20),
+        compiler_params=pltpu.CompilerParams(collective_id=0, has_side_effects=True, vmem_limit_bytes=62 << 20),
         cost_estimate=pl.CostEstimate(flops=2 * T * D * N, bytes_accessed=2 * D * (T + N), transcendentals=T * N),
     )(partials, norm_gain[None, :], head_weight.T, next_ids[None, :], lengths)
     return out, target.reshape(own)

time: 56.9 us -> 55 us (0.967)
  local copies, waits for them, and re-layouts: 4.83 us -> 2.72 us
    unnamed x10 -> x2, local copies, waits for them, and re-layouts: 4.83 us -> 2.72 us
where the time goes in v2:
time: 55 us; the launch traced here: 54.8 us
  Pallas kernels  51.4 us (93%)
  local copies, waits for them, and re-layouts  2.72 us (5%)
  between operations  0.64 us (1%)
    pallas_call x1, Pallas kernels, on_device(): pl.pallas_call(functools.partial(head_kernel, n, X, Z), out_shape=(jax.Sh...  51.4 us
    unnamed x2, local copies, waits for them, and re-layouts  2.72 us

profile of v2, /device:TPU:0, one launch (start us, length us, event | category | flops | bytes accessed | tf_op | source)
XLA Modules:
  0.0 54.8 jit_solution(12330369666382820529)
XLA Ops:
  0.6 51.4 %shard_map.68 = (bf16[8,9504]{1,0:T(8,128)(2,1)}, f32[1,8]{1,0:T(1,128)}) custom-call(bf16[1,128,8192]{2,1,0:T(8,128)(2,1)} %part_ref.1, f32[1,8192]{1,0:T(1,128)} %bitcast.5, bf16[594,8192]{1,0:T(8,128)(2,1)} %bitcast.4, s32[1,128]{1,0:T(1,128)} %bitcast.6, s32[2]{0:T(128)} %len_ref.1), custom_call_target="tpu_custom_call" | custom-call | flops 1245708288 | bytes 11829248 | tf_op jit(solution)/shard_map/pallas_call | solution.py:327
  52.1 1.6 %copy.9 = bf16[8,9504]{1,0:T(8,128)(2,1)} copy(bf16[8,9504]{1,0:T(8,128)(2,1)} %get-tuple-element.8) | data formatting | bytes 304128
  53.7 1.1 %copy.10 = f32[8]{0:T(128)} copy(f32[8]{0:T(128)} %bitcast.7) | data formatting | bytes 64
